TPU v7x, 256 devices: a whole 4x4x8 slice. The times are simulated.
256 devices in a mesh: leaf: 64 (over z, y, core), rows: 4 (over x).
Axes of the slice: x: 4, y: 4, z: 8, core: 2. Of those that a mesh axis runs over, the one named last changes fastest.
Arguments:
- leaf_rhs: float32 [32, 1024, 512], P(None, 'leaf', 'rows'), may hold values from -6 to 6
- top_rhs: float32 [32, 2048], replicated, may hold values from -6 to 6
- leaf_inverse: float32 [1024, 512, 512], P('leaf', 'rows'), may hold values from -2 to 2, as said below
- leaf_below: float32 [1024, 512, 512], P('leaf', 'rows'), may hold values from -0.015625 to 0.015625
- row_map: int32 [1024, 512], P('leaf', 'rows'), may hold values from 0 to 2047
- top_inverse: float32 [4, 512, 512], P(None, 'rows'), may hold values from -2 to 2, as said below
Outputs:
- leaf_solution: float32 [32, 1024, 512], P(None, 'leaf', 'rows')
- top_solution: float32 [32, 2048], replicated
Inputs may be any that keep to these rules, and one draw needn't show every extreme that they name: `leaf_inverse`: lower triangular, diagonal entries positive. `top_inverse`: lower triangular, diagonal entries positive.
All inputs are finite; a program needn't handle non-finite values.
Results may differ from a plain program's by a relative error of at most 0.000068.
Values sent between devices are 32-bit elements; how exact they have to be, the bound alone decides.
A program may use at most 64 MiB of HBM per device.

v0:
```python
import jax
import jax.numpy as jnp
from jax import lax
from jax.sharding import PartitionSpec as P


def on_device(leaf_rhs, top_rhs, leaf_inverse, leaf_below, row_map, top_inverse):
    highest = lax.Precision.HIGHEST
    count_rhs, local_nodes, part_rows = leaf_rhs.shape
    count_top, top_rows, width_top = top_inverse.shape
    top_columns = top_rhs.shape[1]
    columns = leaf_inverse
    solved_part = jnp.einsum(
        "nvw,knw->knv",
        columns,
        lax.all_gather(leaf_rhs, "rows", axis=2, tiled=True),
        precision=highest,
    )
    columns = leaf_below
    below_update = jnp.einsum(
        "nrw,knw->knr",
        columns,
        lax.all_gather(solved_part, "rows", axis=2, tiled=True),
        precision=highest,
    )
    update = (
        jnp.zeros((count_rhs, top_columns), jnp.float32)
        .at[:, row_map.reshape(-1)]
        .add(below_update.reshape(count_rhs, -1))
    )
    update_blocks = update.reshape(count_rhs, count_top, width_top)
    rhs_blocks = top_rhs.reshape(count_rhs, count_top, width_top)
    summed = lax.psum(update_blocks, ("leaf", "rows"))
    top_forward = jnp.einsum("tvs,kts->ktv", top_inverse, rhs_blocks - summed, precision=highest)
    top_term = jnp.einsum("tvs,ktv->kts", top_inverse, top_forward, precision=highest)
    top_solution = lax.psum(top_term, "rows").reshape(count_rhs, top_columns)
    picked_rows = top_solution[:, row_map]
    back_term = jnp.einsum("nrw,knr->knw", leaf_below, picked_rows, precision=highest)
    corrected = solved_part - lax.psum_scatter(back_term, "rows", scatter_dimension=2, tiled=True)
    leaf_term = jnp.einsum("nvw,knv->knw", leaf_inverse, corrected, precision=highest)
    leaf_solution = lax.psum_scatter(leaf_term, "rows", scatter_dimension=2, tiled=True)
    return (leaf_solution, top_solution)


def solution(mesh):
    placed = (
        P(None, "leaf", "rows"),
        P(),
        P("leaf", "rows", None),
        P("leaf", "rows", None),
        P("leaf", "rows"),
        P(None, "rows", None),
    )
    return jax.shard_map(
        on_device,
        mesh=mesh,
        in_specs=placed,
        out_specs=(P(None, "leaf", "rows"), P()),
        check_vma=False,
    )
```

profile of v0, /device:TPU:1, one launch (start us, length us, event | category | flops | bytes accessed | tf_op | source)
XLA Modules:
  0.0 489.4 jit_solution(11045455504359070789)
XLA Ops:
  7.2 0.0 copy-start
  7.2 0.0 copy-start.4
  7.2 0.0 all-gather.3.cloned.1.call-start
  7.2 1.8 copy.12
  9.1 0.0 all-gather.3.cloned.1.call-update
  9.1 0.0 all-gather.5.cloned.1.call-start
  9.1 32.6 %all-gather.3.cloned.1.call-done = f32[32,16,512]{2,0,1:T(8,128)} async-done(((f32[32,16,128]{2,0,1:T(8,128)}), f32[32,16,512]{2,0,1:T(8,128)}) %all-gather.3.cloned.1.call-update) | async-done | bytes 1048592 | tf_op jit(solution)/shard_map/all_gather | solution.py:16
  41.8 7.5 %convolution_bitcast_fusion.4 = f32[32,16,128]{2,0,1:T(8,128)} fusion(f32[32,16,512]{2,0,1:T(8,128)} %all-gather.3.cloned.1.call-done, f32[16,128,512]{2,1,0:T(8,128)} %param.8), kind=kOutput, calls=%fused_computation.6 | convolution fusion | flops 402653184 | bytes 5505024 | tf_op jit(solution)/shard_map/nvw,knw->knv/dot_general | solution.py:13
  49.2 0.0 all-gather.5.cloned.1.call-update
  49.3 0.0 all-reduce.3.cloned.1.call-start
  49.3 0.0 copy-done.4
  49.3 0.0 copy-start.3
  49.3 29.5 %all-gather.5.cloned.1.call-done = f32[32,16,512]{2,0,1:T(8,128)} async-done(((f32[32,16,128]{2,0,1:T(8,128)}), f32[32,16,512]{2,0,1:T(8,128)}) %all-gather.5.cloned.1.call-update) | async-done | bytes 1048592 | tf_op jit(solution)/shard_map/all_gather | solution.py:23
  78.8 6.8 %convolution_bitcast_fusion.3 = f32[16,4,8,128]{3,2,1,0:T(8,128)S(1)} fusion(f32[32,16,512]{2,0,1:T(8,128)} %all-gather.5.cloned.1.call-done, f32[16,128,512]{2,1,0:T(8,128)} %param.9), kind=kOutput, calls=%fused_computation.5 | convolution fusion | flops 402653184 | bytes 5505024 | tf_op jit(solution)/shard_map/nrw,knw->knr/dot_general | solution.py:20
  85.6 0.3 copy.14
  86.0 12.5 %scatter_custom_fusion = f32[32,2048]{0,1:T(8,128)} fusion(s32[2048]{0:T(1024)S(1)} %bitcast.47, f32[2048,32]{1,0:T(8,128)S(1)} %copy.14, f32[]{:T(128)} %constant.3.clone.1), kind=kCustom, calls=%fused_computation.9 | custom fusion | flops 65536 | bytes 262148 | tf_op jit(solution)/shard_map/scatter-add | solution.py:29
  98.5 0.0 all-reduce.3.cloned.1.call-update
  98.5 0.0 all-reduce.5.cloned.1.call-start
  98.5 0.0 copy-done.3
  98.6 0.3 copy.20
  98.9 256.1 %all-reduce.3.cloned.1.call-done = f32[32,4,512]{0,2,1:T(8,128)} async-done(((f32[32,4,512]{0,2,1:T(8,128)}), f32[32,4,512]{0,2,1:T(8,128)}) %all-reduce.3.cloned.1.call-update) | async-done | bytes 262160 | tf_op jit(solution)/shard_map/psum | solution.py:33
  354.9 0.0 copy-done
  354.9 3.0 convolution_bitcast_fusion.5
  358.0 0.7 convolution_bitcast_fusion.2
  358.6 1.4 copy.21
  360.0 0.0 all-reduce.5.cloned.1.call-update
  360.0 0.2 reduce-scatter.3.cloned.1.call-start
  360.3 49.6 %all-reduce.5.cloned.1.call-done = f32[32,2048]{0,1:T(8,128)} async-done(((f32[32,2048]{0,1:T(8,128)}), f32[32,2048]{0,1:T(8,128)}) %all-reduce.5.cloned.1.call-update) | async-done | bytes 262160 | tf_op jit(solution)/shard_map/psum | solution.py:36
  409.9 6.7 %gather_fusion = f32[2048,32]{1,0:T(8,128)S(1)} fusion(f32[32,2048]{0,1:T(8,128)} %all-reduce.5.cloned.1.call-done, s32[2048]{0:T(1024)S(1)} %fusion.5), kind=kCustom, calls=%fused_computation | custom fusion | bytes 532480 | tf_op jit(solution)/shard_map/gather | solution.py:37
  416.6 0.0 copy-start.2
  416.6 5.5 %convolution_bitcast_fusion.1 = f32[32,16,512]{2,0,1:T(8,128)} fusion(f32[32,16,128]{0,2,1:T(8,128)S(1)} %bitcast.44, f32[16,128,512]{2,1,0:T(8,128)} %param.9), kind=kOutput, calls=%fused_computation.3 | convolution fusion | flops 402653184 | bytes 5505024 | tf_op jit(solution)/shard_map/nrw,knr->knw/dot_general | solution.py:38
  422.0 0.0 copy-start.1
  422.0 0.0 reduce-scatter.3.cloned.1.call-update
  422.1 0.0 reduce-scatter.5.cloned.1.call-start
  422.1 27.1 %reduce-scatter.3.cloned.1.call-done = f32[32,16,128]{2,0,1:T(8,128)} async-done(((f32[32,16,512]{2,0,1:T(8,128)}), f32[32,16,128]{2,0,1:T(8,128)}) %reduce-scatter.3.cloned.1.call-update) | async-done | bytes 262160 | tf_op jit(solution)/shard_map/reduce_scatter | solution.py:39
  449.2 0.0 copy-done.2
  449.2 5.6 %convolution_bitcast_fusion = f32[32,16,512]{2,0,1:T(8,128)} fusion(f32[16,128,512]{2,1,0:T(8,128)} %param.8, f32[32,16,128]{2,0,1:T(8,128)S(1)} %copy-done.2, f32[32,16,128]{2,0,1:T(8,128)} %reduce-scatter.3.cloned.1.call-done), kind=kOutput, calls=%fused_computation.2 | convolution fusion | flops 402718720 | bytes 5767168 | tf_op jit(solution)/shard_map/nvw,knv->knw/dot_general | solution.py:40
  454.8 0.0 reduce-scatter.5.cloned.1.call-update
  454.8 0.0 copy-done.1
  454.8 1.0 copy.19
  455.8 24.9 %reduce-scatter.5.cloned.1.call-done = f32[32,16,128]{2,0,1:T(8,128)} async-done(((f32[32,16,512]{2,0,1:T(8,128)}), f32[32,16,128]{2,0,1:T(8,128)}) %reduce-scatter.5.cloned.1.call-update) | async-done | bytes 262160 | tf_op jit(solution)/shard_map/reduce_scatter | solution.py:41
  480.8 1.8 copy.18
  (3 shorter events, 0.0 us)
Async XLA Ops:
  7.2 347.8 %copy-start = (f32[4,128,512]{2,1,0:T(8,128)S(1)}, f32[4,128,512]{2,1,0:T(8,128)}, u32[]{:S(2)}) copy-start(f32[4,128,512]{2,1,0:T(8,128)} %param.11) | copy-start | bytes 3145732
  7.2 42.1 %copy-start.4 = (s32[16,128]{1,0:T(8,128)S(1)}, s32[16,128]{1,0:T(8,128)}, u32[]{:S(2)}) copy-start(s32[16,128]{1,0:T(8,128)} %param.10) | copy-start | bytes 24580
  7.2 34.6 %all-gather.3.cloned.1.call-start = ((), (), s32[]{:S(2)}) async-start(), calls=%async_computation.2 | async-start | bytes 1310720 | tf_op jit(solution)/shard_map/all_gather | solution.py:16
  9.1 69.7 %all-gather.5.cloned.1.call-start = ((), (), s32[]{:S(2)}) async-start(), calls=%async_computation.3 | async-start | bytes 1310720 | tf_op jit(solution)/shard_map/all_gather | solution.py:23
  49.3 305.7 %all-reduce.3.cloned.1.call-start = ((), (), s32[]{:S(2)}) async-start(), calls=%async_computation.4 | async-start | bytes 2097152 | tf_op jit(solution)/shard_map/psum | solution.py:33
  49.3 49.2 %copy-start.3 = (f32[32,2048]{1,0:T(8,128)S(1)}, f32[32,2048]{1,0:T(8,128)}, u32[]{:S(2)}) copy-start(f32[32,2048]{1,0:T(8,128)} %param.7) | copy-start | bytes 786436
  98.5 311.4 %all-reduce.5.cloned.1.call-start = ((), (), s32[]{:S(2)}) async-start(), calls=%async_computation.5 | async-start | bytes 2097152 | tf_op jit(solution)/shard_map/psum | solution.py:36
  360.0 89.2 %reduce-scatter.3.cloned.1.call-start = ((), (), s32[]{:S(2)}) async-start(), calls=%async_computation.6 | async-start | bytes 1310720 | tf_op jit(solution)/shard_map/reduce_scatter | solution.py:39
  416.6 32.6 %copy-start.2 = (f32[32,16,128]{2,0,1:T(8,128)S(1)}, f32[32,16,128]{2,0,1:T(8,128)}, u32[]{:S(2)}) copy-start(f32[32,16,128]{2,0,1:T(8,128)} %convolution_bitcast_fusion.4) | copy-start | bytes 786436
  422.0 32.8 %copy-start.1 = (f32[32,2048]{0,1:T(8,128)S(1)}, f32[32,2048]{0,1:T(8,128)}, u32[]{:S(2)}) copy-start(f32[32,2048]{0,1:T(8,128)} %all-reduce.5.cloned.1.call-done) | copy-start | bytes 786436
  422.1 58.7 %reduce-scatter.5.cloned.1.call-start = ((), (), s32[]{:S(2)}) async-start(), calls=%async_computation.7 | async-start | bytes 1310720 | tf_op jit(solution)/shard_map/reduce_scatter | solution.py:41
Sparse Core Ops, SparseCore 0:
  10.4 31.3 all-gather.2
  49.4 29.3 all-gather.4
  98.6 256.2 all-reduce.2
  360.2 49.6 all-reduce.4
  422.2 26.9 reduce-scatter.2
  454.9 25.8 reduce-scatter.4
where the time goes:
time: 490 us; the launch traced here: 489 us
  waiting for transfers between devices  420 us (86%)
  matrix products  29 us (6%)
  between operations  14.2 us (3%)
  local copies, waits for them, and re-layouts  13.4 us (3%)
  other arithmetic  12.5 us (3%)
    psum x1, waiting for transfers between devices, on_device(): summed = lax.psum(update_blocks, ('leaf', 'rows'))  256 us
    psum x1, waiting for transfers between devices, on_device(): top_solution = lax.psum(top_term, 'rows').reshape(count_rhs, top_columns)  49.6 us
    all_gather x1, waiting for transfers between devices, on_device(): lax.all_gather(leaf_rhs, 'rows', axis=2, tiled=True)  32.6 us
    all_gather x1, waiting for transfers between devices, on_device(): lax.all_gather(solved_part, 'rows', axis=2, tiled=True)  29.5 us
    reduce_scatter x1, waiting for transfers between devices, on_device(): lax.psum_scatter(back_term, 'rows', scatter_dimension=2, tiled=True)  27.1 us
    reduce_scatter x1, waiting for transfers between devices, on_device(): lax.psum_scatter(leaf_term, 'rows', scatter_dimension=2, tiled=True)  24.9 us
    scatter-add x1, other arithmetic, on_device(): update = jnp.zeros((count_rhs, top_columns), jnp.float32).at[:, row_map.r...  12.5 us
  transfers between devices with their start and end apart: 6, of which 6 were waited for; matrix products, arithmetic and copies ran while one was open for 0% of the time, Pallas kernels for 0%

commit v1 on v0

v1 whole, which is shorter than its diff:
```python
import functools

import jax
import jax.numpy as jnp
from jax import lax
from jax.experimental import pallas as pl
from jax.experimental.pallas import tpu as pltpu
from jax.sharding import PartitionSpec as P

F32 = jnp.float32
BF16 = jnp.bfloat16
NT_DIMS = (((1,), (1,)), ((), ()))
NN_DIMS = (((1,), (0,)), ((), ()))

NX = 4
G = 2
LANES = 128

F_SKEW = (0, 1, 3, 5)
B_SKEW = (0, 2, 4, 6, 8)


def split(v):
    hi = v.astype(BF16)
    lo = (v - hi.astype(F32)).astype(BF16)
    return hi, lo


def mm_nt(x, w):
    m = x.shape[0]
    hi, lo = split(x)
    o = lax.dot_general(jnp.concatenate([hi, lo], 0), w, NT_DIMS, preferred_element_type=F32)
    return (o[:m, :LANES] + o[:m, LANES:]) + (o[m:, :LANES] + o[m:, LANES:])


def mm_nn(hi, lo, w):
    m = hi.shape[0]
    top = jnp.concatenate([hi, hi], 1)
    low = jnp.concatenate([lo, lo], 1)
    o = lax.dot_general(jnp.concatenate([top, low], 0), w, NN_DIMS, preferred_element_type=F32)
    return o[:m] + o[m:]


def kernel(
    dims,
    rhs_ref, trhs_ref, map_ref, inv_hbm, below_hbm, tinv_hbm,
    leaf_out, top_out,
    a_f32, b_f32, t_f32, a_hl, b_hl, t_hl, onehot,
    gb, gy, upd, zbuf0, ztop, cbuf, yacc, ybuf, zbuf, xbuf, xbuf2, rvec, hl_in, sol, s_hl,
    pb, pa, r1b, r1a, r2b, r2a,
    in_sem, ssem, rsem, tssem, trsem,
):
    nz, ny = dims
    nodes, k = gb.shape[1], gb.shape[2]
    chunks = nodes // G
    nt = t_f32.shape[0]
    half = zbuf0.shape[0] // 2
    yrows = half // ny
    prow = yrows // nz
    kp = prow // 4
    mp = hl_in.shape[0] // 2

    leaf = lax.axis_index("leaf")
    x = lax.axis_index("rows")
    core = lax.rem(leaf, 2)
    y = lax.rem(leaf // 2, ny)
    z = leaf // (2 * ny)
    right, left = lax.rem(x + 1, NX), lax.rem(x + NX - 1, NX)
    opp = lax.rem(x + 2, NX)

    def leaf_of(zz, yy, cc):
        return (zz * ny + yy) * 2 + cc

    xpeers = [lax.rem(x + d, NX) for d in range(1, NX)]
    ypeers = [lax.rem(y + d, ny) for d in range(1, ny)]
    zpeers = [lax.rem(z + d, nz) for d in range(1, nz)]
    partner = leaf_of(z, y, 1 - core)

    barrier = pltpu.get_barrier_semaphore()
    peers = [{"rows": p} for p in xpeers]
    peers += [{"leaf": leaf_of(z, p, core)} for p in ypeers]
    peers += [{"leaf": leaf_of(p, y, core)} for p in zpeers]
    peers += [{"leaf": partner}]
    for p in peers:
        pl.semaphore_signal(barrier, inc=1, device_id=p, device_id_type=pl.DeviceIdType.MESH)

    def load(which, c):
        src, dst = ((inv_hbm, a_f32), (below_hbm, b_f32))[which]
        return pltpu.make_async_copy(src.at[pl.ds(c * G, G)], dst.at[pl.ds(c * G, G)], in_sem.at[which, c])

    def load_top():
        return pltpu.make_async_copy(tinv_hbm, t_f32, in_sem.at[2, 0])

    for which in range(2):
        def start_load(c, _, which=which):
            load(which, c).start()
            return 0

        lax.fori_loop(0, chunks, start_load, 0)
    load_top().start()

    def fill_own(n, _):
        gb[x, n] = rhs_ref[pl.ds(n, k, stride=nodes), :]
        return 0

    lax.fori_loop(0, nodes, fill_own, 0)

    def send(phase, kind, c, src, dst):
        to = right if kind in (0, 2) else left
        return pltpu.make_async_remote_copy(
            src_ref=src, dst_ref=dst,
            send_sem=ssem.at[phase, kind, c], recv_sem=rsem.at[phase, kind, c],
            device_id={"rows": to}, device_id_type=pl.DeviceIdType.MESH,
        )

    def gather_direct(phase, buf, c, kind):
        blk = buf.at[x, pl.ds(c * G, G)]
        return send(phase, kind, c, blk, blk)

    def gather_forward(phase, buf, c, kind):
        blk = buf.at[left if kind == 2 else right, pl.ds(c * G + (kind - 2), 1)]
        return send(phase, kind, c, blk, blk)

    pl.semaphore_wait(barrier, len(peers))

    def start_rhs(c, _):
        gather_direct(0, gb, c, 0).start()
        gather_direct(0, gb, c, 1).start()
        return 0

    lax.fori_loop(0, chunks, start_rhs, 0)

    for t in range(nt):
        for q in range(4):
            ztop[pl.ds(t * 4 * k + q, k, stride=4), :] = trhs_ref[:, pl.ds((t * 4 + q) * LANES, LANES)]
    upd[...] = jnp.zeros(upd.shape, F32)
    hl_in[...] = jnp.zeros(hl_in.shape, F32)

    def store_split(dst, n, v):
        hi, lo = split(v)
        dst[n, 0:LANES, :] = hi
        dst[n, LANES : 2 * LANES, :] = lo

    def stage(i, skew, body):
        c = i - skew

        @pl.when((c >= 0) & (c < chunks))
        def _():
            body(c)

    def full_row(buf, n):
        return jnp.concatenate([buf[s, n] for s in range(NX)], 1)

    def f0(c):
        load(0, c).wait()
        for j in range(G):
            store_split(a_hl, c * G + j, a_f32[c * G + j])
        gather_direct(0, gb, c, 0).wait_recv()
        gather_forward(0, gb, c, 2).start()
        gather_direct(0, gb, c, 1).wait_recv()
        gather_forward(0, gb, c, 3).start()

    def f1(c):
        gather_forward(0, gb, c, 2).wait_recv()
        gather_forward(0, gb, c, 3).wait_recv()
        for j in range(G):
            n = c * G + j
            gy[x, n] = mm_nt(full_row(gb, n), a_hl[n])
        gather_direct(1, gy, c, 0).start()
        gather_direct(1, gy, c, 1).start()

    def f2(c):
        load(1, c).wait()
        for j in range(G):
            n = c * G + j
            store_split(b_hl, n, b_f32[n])
            row = map_ref[pl.ds(n, 1), :]

            def build(s, _, row=row, j=j):
                cols = lax.broadcasted_iota(jnp.int32, (256, LANES), 0) + s * 256
                hot = jnp.where(cols == row, 1.0, 0.0).astype(BF16)
                onehot[c, pl.ds(pl.multiple_of(s * 256, 256), 256), j * LANES : (j + 1) * LANES] = hot
                return 0

            lax.fori_loop(0, onehot.shape[1] // 256, build, 0)
        gather_direct(1, gy, c, 0).wait_recv()
        gather_forward(1, gy, c, 2).start()
        gather_direct(1, gy, c, 1).wait_recv()
        gather_forward(1, gy, c, 3).start()

    def f3(c):
        gather_forward(1, gy, c, 2).wait_recv()
        gather_forward(1, gy, c, 3).wait_recv()
        u = [mm_nt(full_row(gy, c * G + j), b_hl[c * G + j]) for j in range(G)]
        hi, lo = split(jnp.concatenate(u, 1))
        lhs = jnp.concatenate([hi, lo], 0)
        width = 512
        for s in range(onehot.shape[1] // width):
            o = lax.dot_general(
                lhs, onehot[c, s * width : (s + 1) * width, :], NT_DIMS, preferred_element_type=F32
            )
            upd[:, s * width : (s + 1) * width] += o[:k] + o[k:]

    def forward(i, _):
        stage(i, F_SKEW[0], f0)
        stage(i, F_SKEW[1], f1)
        stage(i, F_SKEW[2], f2)
        stage(i, F_SKEW[3], f3)
        return 0

    lax.fori_loop(0, chunks + F_SKEW[3], forward, 0)

    for t in range(nt):
        for q in range(4):
            zbuf0[pl.ds(t * 4 * k + q, k, stride=4), :] = upd[:, (t * 4 + q) * LANES : (t * 4 + q + 1) * LANES]

    def tsend(step, slot, src, dst, to):
        return pltpu.make_async_remote_copy(
            src_ref=src, dst_ref=dst, send_sem=tssem.at[step, slot], recv_sem=trsem.at[step, slot],
            device_id=to, device_id_type=pl.DeviceIdType.MESH,
        )

    def rows_at(start, size):
        return pl.ds(pl.multiple_of(start, 8), size)

    hand = tsend(0, 0, zbuf0.at[rows_at((1 - core) * half, half)], cbuf, {"leaf": partner})
    hand.start()
    load_top().wait()
    for t in range(nt):
        store_split(t_hl, t, t_f32[t])
    hand.wait_recv()
    yacc[...] = zbuf0[rows_at(core * half, half), :] + cbuf[...]

    ysends = [
        tsend(1, d, yacc.at[rows_at(p * yrows, yrows)], ybuf.at[d], {"leaf": leaf_of(z, p, core)})
        for d, p in enumerate(ypeers)
    ]
    for s in ysends:
        s.start()
    total = yacc[rows_at(y * yrows, yrows), :]
    for d, s in enumerate(ysends):
        s.wait_recv()
        total = total + ybuf[d]
    yacc2 = ybuf.at[ny - 1]
    yacc2[...] = total
    zsends = [
        tsend(2, d, yacc2.at[rows_at(p * prow, prow)], zbuf.at[d], {"leaf": leaf_of(p, y, core)})
        for d, p in enumerate(zpeers)
    ]
    for s in zsends:
        s.start()
    total = yacc2[rows_at(z * prow, prow), :]
    for d, s in enumerate(zsends):
        s.wait_recv()
        total = total + zbuf[d]

    def all_x(step, buf, value):
        buf[x] = value
        sends = [tsend(step, d, buf.at[x], buf.at[x], {"rows": p}) for d, p in enumerate(xpeers)]
        for s in sends:
            s.start()
        for s in sends:
            s.wait_recv()
        return sends, (buf[0] + buf[1]) + (buf[2] + buf[3])

    xsends, total = all_x(3, xbuf, total)
    first = core * half + y * yrows + z * prow
    rvec[...] = ztop[rows_at(first, prow), :] - total
    t_mine = first // (4 * k)
    r = jnp.concatenate([rvec[pl.ds(q, kp, stride=4), :] for q in range(4)], 1)
    hi, lo = split(r)
    hl_in[0:kp, :] = hi.astype(F32)
    hl_in[mp : mp + kp, :] = lo.astype(F32)
    o = lax.dot_general(hl_in[...].astype(BF16), t_hl[t_mine], NT_DIMS, preferred_element_type=F32)
    f = (o[:mp, :LANES] + o[:mp, LANES:]) + (o[mp:, :LANES] + o[mp:, LANES:])
    hi, lo = split(f)
    fhl = jnp.concatenate([hi.astype(F32), lo.astype(F32)], 0)
    fhl = jnp.concatenate([fhl, fhl], 1).astype(BF16)
    o = lax.dot_general(fhl, t_hl[t_mine], NN_DIMS, preferred_element_type=F32)
    s_part = o[:mp] + o[mp:]
    for q in range(4):
        rvec[pl.ds(q, kp, stride=4), :] = s_part[0:kp, q * LANES : (q + 1) * LANES]
    xsends2, total = all_x(4, xbuf2, rvec[...])
    sol[rows_at(first, prow), :] = total

    def spread(step, start, size, targets):
        blk = sol.at[rows_at(start, size)]
        sends = [tsend(step, d, blk, blk, to) for d, to in enumerate(targets)]
        for s in sends:
            s.start()
        for s in sends:
            s.wait_recv()
        return sends

    g1 = spread(5, first, prow, [{"leaf": leaf_of(p, y, core)} for p in zpeers])
    g2 = spread(6, core * half + y * yrows, yrows, [{"leaf": leaf_of(z, p, core)} for p in ypeers])
    g3 = spread(7, core * half, half, [{"leaf": partner}])

    for t in range(nt):
        for q in range(4):
            v = sol[pl.ds(t * 4 * k + q, k, stride=4), :]
            at = (t * 4 + q) * LANES
            top_out[:, at : at + LANES] = v
            hi, lo = split(v)
            s_hl[0:k, at : at + LANES] = hi
            s_hl[k : 2 * k, at : at + LANES] = lo

    def toward_opp(phase, buf, r1, c, kind):
        n = c * G + kind
        return send(phase, kind, c, buf.at[opp, pl.ds(n, 1)], r1.at[pl.ds(n, 1)])

    def toward_next(phase, buf, r2, c, kind):
        ns = pl.ds(c * G, G)
        return send(phase, kind, c, buf.at[right if kind == 2 else left, ns], r2.at[kind - 2, ns])

    def put(buf, n, v):
        for s in range(NX):
            buf[s, n] = v[:, s * LANES : (s + 1) * LANES]

    def start_opp(phase, buf, r1, c):
        toward_opp(phase, buf, r1, c, 0).start()
        toward_opp(phase, buf, r1, c, 1).start()

    def add_and_pass(phase, buf, r1, r2, c):
        n = c * G
        toward_opp(phase, buf, r1, c, 0).wait_recv()
        buf[right, n] += r1[n]
        toward_next(phase, buf, r2, c, 2).start()
        toward_opp(phase, buf, r1, c, 1).wait_recv()
        buf[left, n + 1] += r1[n + 1]
        toward_next(phase, buf, r2, c, 3).start()

    def collect(phase, buf, r2, c):
        toward_next(phase, buf, r2, c, 2).wait_recv()
        toward_next(phase, buf, r2, c, 3).wait_recv()
        ns = pl.ds(c * G, G)
        return buf[x, ns] + (r2[0, ns] + r2[1, ns])

    def b0(c):
        picked = lax.dot_general(s_hl[...], onehot[c], NN_DIMS, preferred_element_type=F32).astype(BF16)
        for j in range(G):
            at = slice(j * LANES, (j + 1) * LANES)
            put(pb, c * G + j, mm_nn(picked[:k, at], picked[k:, at], b_hl[c * G + j]))
        start_opp(2, pb, r1b, c)

    def b1(c):
        add_and_pass(2, pb, r1b, r2b, c)

    def b2(c):
        back = collect(2, pb, r2b, c)
        for j in range(G):
            n = c * G + j
            hi, lo = split(gy[x, n] - back[j])
            put(pa, n, mm_nn(hi, lo, a_hl[n]))
        start_opp(3, pa, r1a, c)

    def b3(c):
        add_and_pass(3, pa, r1a, r2a, c)

    def b4(c):
        done = collect(3, pa, r2a, c)
        for j in range(G):
            leaf_out[pl.ds(c * G + j, k, stride=nodes), :] = done[j]

    def backward(i, _):
        for skew, body in zip(B_SKEW, (b0, b1, b2, b3, b4)):
            stage(i, skew, body)
        return 0

    lax.fori_loop(0, chunks + B_SKEW[4], backward, 0)

    def drain(c, _):
        for phase, buf in ((0, gb), (1, gy)):
            for kind in (0, 1):
                gather_direct(phase, buf, c, kind).wait_send()
                gather_forward(phase, buf, c, kind + 2).wait_send()
        for phase, buf, r1, r2 in ((2, pb, r1b, r2b), (3, pa, r1a, r2a)):
            for kind in (0, 1):
                toward_opp(phase, buf, r1, c, kind).wait_send()
                toward_next(phase, buf, r2, c, kind + 2).wait_send()
        return 0

    lax.fori_loop(0, chunks, drain, 0)
    for s in [hand] + ysends + zsends + xsends + xsends2 + g1 + g2 + g3:
        s.wait_send()


def make(nz, ny):
    def on_device(leaf_rhs, top_rhs, leaf_inverse, leaf_below, row_map, top_inverse):
        k, nodes, width = leaf_rhs.shape
        nt, _, s = top_inverse.shape
        full = leaf_inverse.shape[2]
        cols = top_rhs.shape[1]
        chunks = nodes // G
        rows = cols * k // LANES
        half = rows // 2
        yrows = half // ny
        prow = yrows // nz
        mp = max(8, prow // 4)
        vmem = pl.BlockSpec(memory_space=pltpu.VMEM)
        hbm = pl.BlockSpec(memory_space=pl.ANY)
        blocks = (NX, nodes, k, LANES)
        scratch = [
            pltpu.VMEM(leaf_inverse.shape, F32),
            pltpu.VMEM(leaf_below.shape, F32),
            pltpu.VMEM(top_inverse.shape, F32),
            pltpu.VMEM((nodes, 2 * LANES, full), BF16),
            pltpu.VMEM((nodes, 2 * LANES, full), BF16),
            pltpu.VMEM((nt, 2 * LANES, s), BF16),
            pltpu.VMEM((chunks, cols, G * LANES), BF16),
            pltpu.VMEM(blocks, F32),
            pltpu.VMEM(blocks, F32),
            pltpu.VMEM((k, cols), F32),
            pltpu.VMEM((rows, LANES), F32),
            pltpu.VMEM((rows, LANES), F32),
            pltpu.VMEM((half, LANES), F32),
            pltpu.VMEM((half, LANES), F32),
            pltpu.VMEM((ny, yrows, LANES), F32),
            pltpu.VMEM((nz, prow, LANES), F32),
            pltpu.VMEM((NX, prow, LANES), F32),
            pltpu.VMEM((NX, prow, LANES), F32),
            pltpu.VMEM((prow, LANES), F32),
            pltpu.VMEM((2 * mp, s), F32),
            pltpu.VMEM((rows, LANES), F32),
            pltpu.VMEM((2 * k, cols), BF16),
            pltpu.VMEM(blocks, F32),
            pltpu.VMEM(blocks, F32),
            pltpu.VMEM(blocks[1:], F32),
            pltpu.VMEM(blocks[1:], F32),
            pltpu.VMEM((2,) + blocks[1:], F32),
            pltpu.VMEM((2,) + blocks[1:], F32),
            pltpu.SemaphoreType.DMA((3, chunks)),
            pltpu.SemaphoreType.DMA((4, 4, chunks)),
            pltpu.SemaphoreType.DMA((4, 4, chunks)),
            pltpu.SemaphoreType.DMA((8, 8)),
            pltpu.SemaphoreType.DMA((8, 8)),
        ]
        macs = nodes * width * full * k
        leaf_solution, top_solution = pl.pallas_call(
            functools.partial(kernel, (nz, ny)),
            out_shape=(
                jax.ShapeDtypeStruct((k * nodes, width), F32),
                jax.ShapeDtypeStruct((k, cols), F32),
            ),
            in_specs=[vmem, vmem, vmem, hbm, hbm, hbm],
            out_specs=(vmem, vmem),
            scratch_shapes=scratch,
            compiler_params=pltpu.CompilerParams(
                collective_id=0, has_side_effects=True, vmem_limit_bytes=52 * 2**20
            ),
            cost_estimate=pl.CostEstimate(flops=24 * macs, bytes_accessed=10 * 2**20, transcendentals=0),
        )(
            leaf_rhs.reshape(k * nodes, width),
            top_rhs,
            row_map,
            leaf_inverse,
            leaf_below,
            top_inverse,
        )
        return leaf_solution.reshape(k, nodes, width), top_solution

    return on_device


def solution(mesh, nz=8, ny=4):
    placed = (
        P(None, "leaf", "rows"),
        P(),
        P("leaf", "rows", None),
        P("leaf", "rows", None),
        P("leaf", "rows"),
        P(None, "rows", None),
    )
    return jax.shard_map(
        make(nz, ny),
        mesh=mesh,
        in_specs=placed,
        out_specs=(P(None, "leaf", "rows"), P()),
        check_vma=False,
    )
```

time: 490 us -> 99.6 us (0.20)
  waiting for transfers between devices: 420 us -> 0 us
  Pallas kernels: 0 us -> 94.4 us
  matrix products: 29 us -> 0 us
  between operations: 14.2 us -> 0.65 us
  other arithmetic: 12.5 us -> 0 us
  local copies, waits for them, and re-layouts: 13.4 us -> 4 us
    psum x2 -> x0, waiting for transfers between devices: 306 us -> none  [the longest x1 256 us: on_device(): summed = lax.psum(update_blocks, ('leaf', 'rows'))]
    pallas_call x0 -> x1, Pallas kernels: none -> 94.4 us  [on_device(): pl.pallas_call(functools.partial(kernel, (nz, ny)), out_shape=(jax.ShapeD...]
    all_gather x2 -> x0, waiting for transfers between devices: 62.1 us -> none  [the longest x1 32.6 us: on_device(): lax.all_gather(leaf_rhs, 'rows', axis=2, tiled=True)]
    reduce_scatter x2 -> x0, waiting for transfers between devices: 52 us -> none  [the longest x1 27.1 us: on_device(): lax.psum_scatter(back_term, 'rows', scatter_dimension=2, tiled=True)]
    dot_general x6 -> x0, matrix products: 29 us -> none  [the longest x1 7.48 us: on_device(): jnp.einsum('nvw,knw->knv', columns, lax.all_gather(leaf_rhs, 'rows', axis...]
    scatter-add x1 -> x0, other arithmetic: 12.5 us -> none  [on_device(): update = jnp.zeros((count_rhs, top_columns), jnp.float32).at[:, row_map.r...]
    gather x1 -> x0, local copies, waits for them, and re-layouts: 6.68 us -> none  [on_device(): picked_rows = top_solution[:, row_map]]
  transfers between devices with their start and end apart: 6 -> 0, of which waited for: 6 -> 0; matrix products, arithmetic and copies ran while one was open for 0% -> 0% of each run, Pallas kernels for 0% -> 0%
where the time goes in v1:
time: 99.6 us; the launch traced here: 99.1 us
  Pallas kernels  94.4 us (95%)
  local copies, waits for them, and re-layouts  4 us (4%)
    pallas_call x1, Pallas kernels, on_device(): pl.pallas_call(functools.partial(kernel, (nz, ny)), out_shape=(jax.ShapeD...  94.4 us
    unnamed x8, local copies, waits for them, and re-layouts  4 us

profile of v1, /device:TPU:1, one launch (start us, length us, event | category | flops | bytes accessed | tf_op | source)
XLA Modules:
  0.0 99.1 jit_solution(17707479089881903806)
XLA Ops:
  0.6 0.0 copy-start
  0.6 0.9 copy-done
  1.6 0.0 copy-start.1
  1.6 0.9 copy-done.1
  2.5 0.0 copy-start.2
  2.5 0.7 copy-done.2
  3.2 94.4 %shard_map.77 = (f32[512,128]{1,0:T(8,128)S(1)}, f32[32,2048]{1,0:T(8,128)S(1)}) custom-call(f32[512,128]{1,0:T(8,128)S(1)} %bitcast.2, f32[32,2048]{1,0:T(8,128)S(1)} %copy-done.1, s32[16,128]{1,0:T(8,128)S(1)} %copy-done.2, f32[16,128,512]{2,1,0:T(8,128)} %inv_hbm.1, f32[16,128,512]{2,1,0:T(8,128)} %below_hbm.1, f32[4,128,512]{2,1,0:T(8,128)} %tinv_hbm.1), custom_call_target="tpu_custom_call" | custom-call | flops 805306368 | bytes 10485760 | tf_op jit(solution)/shard_map/pallas_call | solution.py:439
  97.7 0.7 copy.10
  98.4 0.7 copy.11
Async XLA Ops:
  0.6 1.0 copy-start
  1.6 0.9 copy-start.1
  2.5 0.7 copy-start.2

commit v2 on v0

v2 whole, which is shorter than its diff:
```python
import functools

import jax
import jax.numpy as jnp
from jax import lax
from jax.experimental import pallas as pl
from jax.experimental.pallas import tpu as pltpu
from jax.sharding import PartitionSpec as P

F32 = jnp.float32
BF16 = jnp.bfloat16
NT_DIMS = (((1,), (1,)), ((), ()))
NN_DIMS = (((1,), (0,)), ((), ()))

NX = 4
G = 4
LANES = 128
H = 2

F_AT = (0, 3, 6, 9)
F_GAP = 3
TOP_AT = ((1, 4, 8, 9, 10, 11, 12), (8, 9, 10, 11, 12, 14, 16))
TAKE_AT = (17, 13)
B_FIRST = 13
B_AT = (0, 3, 6, 9, 12)
B_GAP = 0
STRAIGHT = ((0, 0), (6, 8), (0, 0), (6, 8))
PREP = 4


def split(v):
    hi = v.astype(BF16)
    lo = (v - hi.astype(F32)).astype(BF16)
    return hi, lo


def mm_row(x, w):
    m = x.shape[0]
    hi, lo = split(x)
    o = lax.dot_general(jnp.concatenate([hi, lo], 0), w, NN_DIMS, preferred_element_type=F32)
    return (o[:m, :LANES] + o[:m, LANES:]) + (o[m:, :LANES] + o[m:, LANES:])


def mm_nn(hi, lo, w):
    m = hi.shape[0]
    top = jnp.concatenate([hi, hi], 1)
    low = jnp.concatenate([lo, lo], 1)
    o = lax.dot_general(jnp.concatenate([top, low], 0), w, NN_DIMS, preferred_element_type=F32)
    return o[:m] + o[m:]


def kernel(
    dims,
    rhs_hbm, trhs_hbm, map_hbm, inv_hbm, below_hbm, tinv_hbm,
    leaf_out, top_out,
    rhs_ref, trhs_ref, map_ref, a_f32, b_f32, t_f32, a_hl, b_hl, t_hl, a_t, b_t, hot_in, hot_out,
    gb, gy, upd, urow, ztop, cbuf, yacc, ybuf, zbuf, xbuf, xbuf2, rvec, hl_in, sol, s_hl,
    pb, pa, r1b, r1a, r2b, r2a,
    in_sem, ssem, rsem, tssem, trsem,
):
    nz, ny = dims
    nodes, k = gb.shape[2], gb.shape[3]
    chunks = nodes // G
    units = H * chunks
    nt = t_f32.shape[0]
    cols = upd.shape[2]
    yrows = urow.shape[1] // ny
    prow = yrows // nz
    kp = prow // 4
    mp = hl_in.shape[0] // 2

    leaf = lax.axis_index("leaf")
    x = lax.axis_index("rows")
    core = lax.rem(leaf, 2)
    y = lax.rem(leaf // 2, ny)
    z = leaf // (2 * ny)
    right, left = lax.rem(x + 1, NX), lax.rem(x + NX - 1, NX)
    opp = lax.rem(x + 2, NX)

    def leaf_of(zz, yy, cc):
        return (zz * ny + yy) * 2 + cc

    xpeers = [lax.rem(x + d, NX) for d in range(1, NX)]
    ypeers = [lax.rem(y + d, ny) for d in range(1, ny)]
    zpeers = [lax.rem(z + d, nz) for d in range(1, nz)]
    partner = leaf_of(z, y, 1 - core)

    barrier = pltpu.get_barrier_semaphore()
    peers = [{"rows": p} for p in xpeers]
    peers += [{"leaf": leaf_of(z, p, core)} for p in ypeers]
    peers += [{"leaf": leaf_of(p, y, core)} for p in zpeers]
    peers += [{"leaf": partner}]
    for p in peers:
        pl.semaphore_signal(barrier, inc=1, device_id=p, device_id_type=pl.DeviceIdType.MESH)

    def load(which, c):
        src, dst = ((inv_hbm, a_f32), (below_hbm, b_f32))[which]
        return pltpu.make_async_copy(src.at[pl.ds(c * G, G)], dst.at[pl.ds(c * G, G)], in_sem.at[which, c])

    whole = [
        pltpu.make_async_copy(src, dst, in_sem.at[2, i])
        for i, (src, dst) in enumerate(
            ((rhs_hbm, rhs_ref), (map_hbm, map_ref), (tinv_hbm, t_f32), (trhs_hbm, trhs_ref))
        )
    ]
    whole[0].start()
    whole[1].start()
    for which in range(2):
        def start_load(c, _, which=which):
            load(which, c).start()
            return 0

        lax.fori_loop(0, chunks, start_load, 0)
    whole[2].start()
    whole[3].start()
    whole[0].wait()

    def fill_own(n, _):
        for h in range(H):
            gb[x, h, n] = rhs_ref[pl.ds(h * k * nodes + n, k, stride=nodes), :]
        return 0

    lax.fori_loop(0, nodes, fill_own, 0)

    def store_split(dst, n, v):
        hi, lo = split(v)
        dst[n, 0:LANES, :] = hi
        dst[n, LANES : 2 * LANES, :] = lo

    def store_both(dst, dst_t, n, v):
        hi, lo = split(v)
        dst[n, 0:LANES, :] = hi
        dst[n, LANES : 2 * LANES, :] = lo
        dst_t[n, :, 0:LANES] = hi.T
        dst_t[n, :, LANES : 2 * LANES] = lo.T

    def prepare(c, _):
        load(0, c).wait()
        for j in range(G):
            store_both(a_hl, a_t, c * G + j, a_f32[c * G + j])
        return 0

    def prepare_below(c, _):
        load(1, c).wait()
        for j in range(G):
            store_both(b_hl, b_t, c * G + j, b_f32[c * G + j])
        for j in range(G):
            own = jnp.broadcast_to(map_ref[pl.ds(c * G + j, 1), :], (LANES, LANES)).T
            at = lax.broadcasted_iota(jnp.int32, (LANES, LANES), 1)
            for q in range(cols // LANES):
                hot = jnp.where(own == at + q * LANES, 1.0, 0.0).astype(BF16)
                hot_in[c, j * LANES : (j + 1) * LANES, q * LANES : (q + 1) * LANES] = hot
        return 0

    def prepare_out(u):
        for j in range(G):
            row = map_ref[pl.ds(u * G + j, 1), :]

            def build(s, _, row=row, j=j):
                at = lax.broadcasted_iota(jnp.int32, (256, LANES), 0) + s * 256
                hot = jnp.where(at == row, 1.0, 0.0).astype(BF16)
                hot_out[u, pl.ds(pl.multiple_of(s * 256, 256), 256), j * LANES : (j + 1) * LANES] = hot
                return 0

            lax.fori_loop(0, cols // 256, build, 0)

    whole[1].wait()
    lax.fori_loop(0, PREP, prepare, 0)

    def send(phase, kind, u, src, dst):
        to = opp if kind == 4 else right if kind in (0, 2) else left
        return pltpu.make_async_remote_copy(
            src_ref=src, dst_ref=dst,
            send_sem=ssem.at[phase, kind, u], recv_sem=rsem.at[phase, kind, u],
            device_id={"rows": to}, device_id_type=pl.DeviceIdType.MESH,
        )

    def place(u):
        return lax.div(u, chunks), lax.rem(u, chunks)

    def straight(phase, u):
        low, high = STRAIGHT[phase]
        return (u >= low) & (u < high)

    def gather_direct(phase, u, kind):
        h, c = place(u)
        blk = (gb, gy)[phase].at[x, h, pl.ds(c * G, G)]
        return send(phase, kind, u, blk, blk)

    def gather_forward(phase, u, kind):
        h, c = place(u)
        blk = (gb, gy)[phase].at[left if kind == 2 else right, h, pl.ds(c * G + (kind - 2) * (G // 2), G // 2)]
        return send(phase, kind, u, blk, blk)

    def gather_start(phase, u):
        gather_direct(phase, u, 0).start()
        gather_direct(phase, u, 1).start()

        @pl.when(straight(phase, u))
        def _():
            gather_direct(phase, u, 4).start()

    def gather_pass(phase, u):
        for kind in (0, 1):
            gather_direct(phase, u, kind).wait_recv()

            @pl.when(jnp.logical_not(straight(phase, u)))
            def _(kind=kind):
                gather_forward(phase, u, kind + 2).start()

    def gather_end(phase, u, finish):
        @pl.when(straight(phase, u))
        def _():
            finish(gather_direct(phase, u, 4))

        @pl.when(jnp.logical_not(straight(phase, u)))
        def _():
            finish(gather_forward(phase, u, 2))
            finish(gather_forward(phase, u, 3))

    def arrive(copy):
        copy.wait_recv()

    def leave(copy):
        copy.wait_send()

    pl.semaphore_wait(barrier, len(peers))

    def start_rhs(u, _):
        gather_start(0, u)
        return 0

    lax.fori_loop(0, chunks, start_rhs, 0)

    lax.fori_loop(PREP, chunks, prepare, 0)
    lax.fori_loop(0, chunks, prepare_below, 0)
    whole[2].wait()
    for t in range(nt):
        store_split(t_hl, t, t_f32[t])
    whole[3].wait()
    for t in range(nt):
        for q in range(4):
            at = (t * 4 + q) * LANES
            ztop[pl.ds(t * 4 * k + q, k, stride=4), :] = trhs_ref[
                pl.ds(pl.multiple_of(core * k, 8), k), at : at + LANES
            ]
    upd[...] = jnp.zeros(upd.shape, F32)
    hl_in[...] = jnp.zeros(hl_in.shape, F32)

    def full_row(buf, h, n):
        return jnp.concatenate([buf[s, h, n] for s in range(NX)], 1)

    def tsend(step, slot, src, dst, to):
        return pltpu.make_async_remote_copy(
            src_ref=src, dst_ref=dst, send_sem=tssem.at[step, slot], recv_sem=trsem.at[step, slot],
            device_id=to, device_id_type=pl.DeviceIdType.MESH,
        )

    def rows_at(start, size):
        return pl.ds(pl.multiple_of(start, 8), size)

    def f0(u):
        gather_pass(0, u)

    def f1(u):
        h, c = place(u)
        gather_end(0, u, arrive)
        for j in range(G):
            n = c * G + j
            gy[x, h, n] = mm_row(full_row(gb, h, n), a_t[n])
        gather_start(1, u)

        @pl.when(u + chunks < units)
        def _():
            gather_start(0, u + chunks)

    def f2(u):
        gather_pass(1, u)

    hand = tsend(0, 0, urow.at[1 - core], cbuf, {"leaf": partner})

    def f3(u):
        h, c = place(u)
        gather_end(1, u, arrive)
        v = [mm_row(full_row(gy, h, c * G + j), b_t[c * G + j]) for j in range(G)]
        hi, lo = split(jnp.concatenate(v, 1))
        lhs = jnp.concatenate([hi, lo], 0)
        width = 512
        for s in range(cols // width):
            o = lax.dot_general(
                lhs, hot_in[c, :, s * width : (s + 1) * width], NN_DIMS, preferred_element_type=F32
            )
            upd[h, :, s * width : (s + 1) * width] += o[:k] + o[k:]

        @pl.when(c == chunks - 1)
        def _():
            for t in range(nt):
                for q in range(4):
                    at = (t * 4 + q) * LANES
                    urow[h, pl.ds(t * 4 * k + q, k, stride=4), :] = upd[h, :, at : at + LANES]

            @pl.when(core != h)
            def _():
                hand.start()

    first = y * yrows + z * prow
    t_mine = first // (4 * k)
    ysends = [
        tsend(1, d, yacc.at[rows_at(p * yrows, yrows)], ybuf.at[d], {"leaf": leaf_of(z, p, core)})
        for d, p in enumerate(ypeers)
    ]
    ysum = ybuf.at[ny - 1]
    zsends = [
        tsend(2, d, ysum.at[rows_at(p * prow, prow)], zbuf.at[d], {"leaf": leaf_of(p, y, core)})
        for d, p in enumerate(zpeers)
    ]
    xsends = [tsend(3, d, xbuf.at[x], xbuf.at[x], {"rows": p}) for d, p in enumerate(xpeers)]
    xsends2 = [tsend(4, d, xbuf2.at[x], xbuf2.at[x], {"rows": p}) for d, p in enumerate(xpeers)]
    sol_z = sol.at[core, rows_at(first, prow)]
    sol_y = sol.at[core, rows_at(y * yrows, yrows)]
    zback = [tsend(5, d, sol_z, sol_z, {"leaf": leaf_of(p, y, core)}) for d, p in enumerate(zpeers)]
    yback = [tsend(6, d, sol_y, sol_y, {"leaf": leaf_of(z, p, core)}) for d, p in enumerate(ypeers)]
    give = tsend(7, 0, sol.at[core], sol.at[core], {"leaf": partner})

    def begin(sends):
        for s in sends:
            s.start()

    def t0():
        hand.wait_recv()
        yacc[...] = urow[core] + cbuf[...]
        begin(ysends)

    def t1():
        total = yacc[rows_at(y * yrows, yrows), :]
        for d, s in enumerate(ysends):
            s.wait_recv()
            total = total + ybuf[d]
        ysum[...] = total
        begin(zsends)

    def t2():
        total = ysum[rows_at(z * prow, prow), :]
        for d, s in enumerate(zsends):
            s.wait_recv()
            total = total + zbuf[d]
        xbuf[x] = total
        begin(xsends)

    def t3():
        for s in xsends:
            s.wait_recv()
        rvec[...] = ztop[rows_at(first, prow), :] - ((xbuf[0] + xbuf[1]) + (xbuf[2] + xbuf[3]))
        r = jnp.concatenate([rvec[pl.ds(q, kp, stride=4), :] for q in range(4)], 1)
        hi, lo = split(r)
        hl_in[0:kp, :] = hi.astype(F32)
        hl_in[mp : mp + kp, :] = lo.astype(F32)
        o = lax.dot_general(hl_in[...].astype(BF16), t_hl[t_mine], NT_DIMS, preferred_element_type=F32)
        f = (o[:mp, :LANES] + o[:mp, LANES:]) + (o[mp:, :LANES] + o[mp:, LANES:])
        hi, lo = split(f)
        fhl = jnp.concatenate([hi.astype(F32), lo.astype(F32)], 0)
        fhl = jnp.concatenate([fhl, fhl], 1).astype(BF16)
        o = lax.dot_general(fhl, t_hl[t_mine], NN_DIMS, preferred_element_type=F32)
        s_part = o[:mp] + o[mp:]
        for q in range(4):
            rvec[pl.ds(q, kp, stride=4), :] = s_part[0:kp, q * LANES : (q + 1) * LANES]
        xbuf2[x] = rvec[...]
        begin(xsends2)

    def t4():
        for s in xsends2:
            s.wait_recv()
        sol[core, rows_at(first, prow), :] = (xbuf2[0] + xbuf2[1]) + (xbuf2[2] + xbuf2[3])
        begin(zback)

    def t5():
        for s in zback:
            s.wait_recv()
        begin(yback)

    def t6():
        for s in yback:
            s.wait_recv()
        give.start()
        unpack(core)

    def take():
        tsend(7, 0, sol.at[1 - core], sol.at[1 - core], {"leaf": partner}).wait_recv()
        unpack(1 - core)

    def unpack(h):
        for t in range(nt):
            for q in range(4):
                v = sol[h, pl.ds(t * 4 * k + q, k, stride=4), :]
                at = (t * 4 + q) * LANES
                top_out[pl.ds(pl.multiple_of(h * k, 8), k), at : at + LANES] = v
                hi, lo = split(v)
                s_hl[h, 0:k, at : at + LANES] = hi
                s_hl[h, k : 2 * k, at : at + LANES] = lo

    def toward_opp(phase, u, kind):
        h, c = place(u)
        ns = pl.ds(c * G + kind * (G // 2), G // 2)
        buf, r1 = ((pb, r1b), (pa, r1a))[phase - 2]
        return send(phase, kind, u, buf.at[opp, h, ns], r1.at[h, ns])

    def toward_next(phase, u, kind):
        h, c = place(u)
        ns = pl.ds(c * G, G)
        buf, r2 = ((pb, r2b), (pa, r2a))[phase - 2]
        return send(phase, kind, u, buf.at[(right, left, opp)[kind - 2], h, ns], r2.at[kind - 2, h, ns])

    def put(buf, h, n, v):
        for s in range(NX):
            buf[s, h, n] = v[:, s * LANES : (s + 1) * LANES]

    def reduce_start(phase, u):
        @pl.when(straight(phase, u))
        def _():
            for kind in (2, 3, 4):
                toward_next(phase, u, kind).start()

        @pl.when(jnp.logical_not(straight(phase, u)))
        def _():
            toward_opp(phase, u, 0).start()
            toward_opp(phase, u, 1).start()

    def reduce_pass(phase, u):
        @pl.when(jnp.logical_not(straight(phase, u)))
        def _():
            h, c = place(u)
            buf, r1 = ((pb, r1b), (pa, r1a))[phase - 2]
            for kind, to in ((0, right), (1, left)):
                ns = pl.ds(c * G + kind * (G // 2), G // 2)
                toward_opp(phase, u, kind).wait_recv()
                buf[to, h, ns] += r1[h, ns]
                toward_next(phase, u, kind + 2).start()

    def reduce_end(phase, u):
        h, c = place(u)
        buf, r2 = ((pb, r2b), (pa, r2a))[phase - 2]
        ns = pl.ds(c * G, G)

        @pl.when(straight(phase, u))
        def _():
            toward_next(phase, u, 4).wait_recv()
            buf[x, h, ns] += r2[2, h, ns]

        toward_next(phase, u, 2).wait_recv()
        toward_next(phase, u, 3).wait_recv()
        return buf[x, h, ns] + (r2[0, h, ns] + r2[1, h, ns])

    def b0(u):
        h, c = place(u)
        picked = lax.dot_general(s_hl[h], hot_out[c], NN_DIMS, preferred_element_type=F32).astype(BF16)
        for j in range(G):
            at = slice(j * LANES, (j + 1) * LANES)
            put(pb, h, c * G + j, mm_nn(picked[:k, at], picked[k:, at], b_hl[c * G + j]))
        reduce_start(2, u)

    def b1(u):
        reduce_pass(2, u)

    def b2(u):
        h, c = place(u)
        back = reduce_end(2, u)
        for j in range(G):
            n = c * G + j
            hi, lo = split(gy[x, h, n] - back[j])
            put(pa, h, n, mm_nn(hi, lo, a_hl[n]))
        reduce_start(3, u)

    def b3(u):
        reduce_pass(3, u)

    def b4(u):
        h, c = place(u)
        done = reduce_end(3, u)
        for j in range(G):
            leaf_out[pl.ds(h * k * nodes + c * G + j, k, stride=nodes), :] = done[j]

    def leave_forward(u):
        for phase in (0, 1):
            gather_direct(phase, u, 0).wait_send()
            gather_direct(phase, u, 1).wait_send()
            gather_end(phase, u, leave)

    base = F_AT[3] + chunks - 1
    b_base = base + B_FIRST

    def step(i, _):
        def unit_at(at, gap, body):
            v = i - at
            second = v >= chunks + gap

            @pl.when(((v >= 0) & (v < chunks)) | (second & (v < units + gap)))
            def _():
                body(jnp.where(second, v - gap, v))

        for j, body in enumerate((t0, t1, t2, t3, t4, t5, t6)):
            pl.when(i == base + jnp.where(core == 0, TOP_AT[0][j], TOP_AT[1][j]))(body)
        pl.when(i == base + jnp.where(core == 0, TAKE_AT[0], TAKE_AT[1]))(take)
        unit_at(F_AT[0], F_GAP, f0)
        unit_at(F_AT[2], F_GAP, f2)
        unit_at(F_AT[1], F_GAP, f1)
        unit_at(F_AT[3], F_GAP, f3)
        unit_at(b_base + B_AT[1], B_GAP, b1)
        unit_at(b_base + B_AT[3], B_GAP, b3)
        unit_at(b_base + B_AT[4], B_GAP, b4)
        unit_at(b_base + B_AT[2], B_GAP, b2)
        unit_at(b_base + B_AT[0], B_GAP, b0)
        unit_at(base + TOP_AT[0][2], 0, leave_forward)
        pl.when((i > base) & (i <= base + chunks))(lambda: prepare_out(i - base - 1))
        return 0

    lax.fori_loop(0, b_base + B_AT[4] + units + B_GAP, step, 0)

    def drain(u, _):
        for phase in (2, 3):
            toward_next(phase, u, 2).wait_send()
            toward_next(phase, u, 3).wait_send()

            @pl.when(straight(phase, u))
            def _(phase=phase):
                toward_next(phase, u, 4).wait_send()

            @pl.when(jnp.logical_not(straight(phase, u)))
            def _(phase=phase):
                toward_opp(phase, u, 0).wait_send()
                toward_opp(phase, u, 1).wait_send()

        return 0

    lax.fori_loop(0, units, drain, 0)
    for s in [hand, give] + ysends + zsends + xsends + xsends2 + zback + yback:
        s.wait_send()


def make(nz, ny):
    def on_device(leaf_rhs, top_rhs, leaf_inverse, leaf_below, row_map, top_inverse):
        k, nodes, width = leaf_rhs.shape
        nt, _, s = top_inverse.shape
        full = leaf_inverse.shape[2]
        cols = top_rhs.shape[1]
        chunks = nodes // G
        rows = cols * k // LANES
        half = rows // H
        kh = k // H
        units = H * chunks
        yrows = half // ny
        prow = yrows // nz
        mp = max(8, prow // 4)
        vmem = pl.BlockSpec(memory_space=pltpu.VMEM)
        hbm = pl.BlockSpec(memory_space=pltpu.HBM)
        blocks = (NX, H, nodes, kh, LANES)
        scratch = [
            pltpu.VMEM((k * nodes, width), F32),
            pltpu.VMEM((k, cols), F32),
            pltpu.VMEM((nodes, width), jnp.int32),
            pltpu.VMEM(leaf_inverse.shape, F32),
            pltpu.VMEM(leaf_below.shape, F32),
            pltpu.VMEM(top_inverse.shape, F32),
            pltpu.VMEM((nodes, 2 * LANES, full), BF16),
            pltpu.VMEM((nodes, 2 * LANES, full), BF16),
            pltpu.VMEM((nt, 2 * LANES, s), BF16),
            pltpu.VMEM((nodes, full, 2 * LANES), BF16),
            pltpu.VMEM((nodes, full, 2 * LANES), BF16),
            pltpu.VMEM((chunks, G * LANES, cols), BF16),
            pltpu.VMEM((chunks, cols, G * LANES), BF16),
            pltpu.VMEM(blocks, F32),
            pltpu.VMEM(blocks, F32),
            pltpu.VMEM((H, kh, cols), F32),
            pltpu.VMEM((H, half, LANES), F32),
            pltpu.VMEM((half, LANES), F32),
            pltpu.VMEM((half, LANES), F32),
            pltpu.VMEM((half, LANES), F32),
            pltpu.VMEM((ny, yrows, LANES), F32),
            pltpu.VMEM((nz, prow, LANES), F32),
            pltpu.VMEM((NX, prow, LANES), F32),
            pltpu.VMEM((NX, prow, LANES), F32),
            pltpu.VMEM((prow, LANES), F32),
            pltpu.VMEM((2 * mp, s), F32),
            pltpu.VMEM((H, half, LANES), F32),
            pltpu.VMEM((H, 2 * kh, cols), BF16),
            pltpu.VMEM(blocks, F32),
            pltpu.VMEM(blocks, F32),
            pltpu.VMEM(blocks[1:], F32),
            pltpu.VMEM(blocks[1:], F32),
            pltpu.VMEM((3,) + blocks[1:], F32),
            pltpu.VMEM((3,) + blocks[1:], F32),
            pltpu.SemaphoreType.DMA((3, max(chunks, 4))),
            pltpu.SemaphoreType.DMA((4, 5, units)),
            pltpu.SemaphoreType.DMA((4, 5, units)),
            pltpu.SemaphoreType.DMA((8, 8)),
            pltpu.SemaphoreType.DMA((8, 8)),
        ]
        macs = nodes * width * full * k
        leaf_solution, top_solution = pl.pallas_call(
            functools.partial(kernel, (nz, ny)),
            out_shape=(
                jax.ShapeDtypeStruct((k * nodes, width), F32),
                jax.ShapeDtypeStruct((k, cols), F32),
            ),
            in_specs=[hbm] * 6,
            out_specs=(vmem, vmem),
            scratch_shapes=scratch,
            compiler_params=pltpu.CompilerParams(
                collective_id=0, has_side_effects=True, vmem_limit_bytes=60 * 2**20
            ),
            cost_estimate=pl.CostEstimate(flops=24 * macs, bytes_accessed=10 * 2**20, transcendentals=0),
        )(
            leaf_rhs.reshape(k * nodes, width),
            top_rhs,
            row_map,
            leaf_inverse,
            leaf_below,
            top_inverse,
        )
        return leaf_solution.reshape(k, nodes, width), top_solution

    return on_device


def solution(mesh, nz=8, ny=4):
    placed = (
        P(None, "leaf", "rows"),
        P(),
        P("leaf", "rows", None),
        P("leaf", "rows", None),
        P("leaf", "rows"),
        P(None, "rows", None),
    )
    return jax.shard_map(
        make(nz, ny),
        mesh=mesh,
        in_specs=placed,
        out_specs=(P(None, "leaf", "rows"), P()),
        check_vma=False,
    )
```

time: 490 us -> 88.4 us (0.18)
  waiting for transfers between devices: 420 us -> 0 us
  Pallas kernels: 0 us -> 84.3 us
  matrix products: 29 us -> 0 us
  between operations: 14.2 us -> 0.64 us
  other arithmetic: 12.5 us -> 0 us
  local copies, waits for them, and re-layouts: 13.4 us -> 3.34 us
    psum x2 -> x0, waiting for transfers between devices: 306 us -> none  [the longest x1 256 us: on_device(): summed = lax.psum(update_blocks, ('leaf', 'rows'))]
    pallas_call x0 -> x1, Pallas kernels: none -> 84.3 us  [on_device(): pl.pallas_call(functools.partial(kernel, (nz, ny)), out_shape=(jax.ShapeD...]
    all_gather x2 -> x0, waiting for transfers between devices: 62.1 us -> none  [the longest x1 32.6 us: on_device(): lax.all_gather(leaf_rhs, 'rows', axis=2, tiled=True)]
    reduce_scatter x2 -> x0, waiting for transfers between devices: 52 us -> none  [the longest x1 27.1 us: on_device(): lax.psum_scatter(back_term, 'rows', scatter_dimension=2, tiled=True)]
    dot_general x6 -> x0, matrix products: 29 us -> none  [the longest x1 7.48 us: on_device(): jnp.einsum('nvw,knw->knv', columns, lax.all_gather(leaf_rhs, 'rows', axis...]
    scatter-add x1 -> x0, other arithmetic: 12.5 us -> none  [on_device(): update = jnp.zeros((count_rhs, top_columns), jnp.float32).at[:, row_map.r...]
    gather x1 -> x0, local copies, waits for them, and re-layouts: 6.68 us -> none  [on_device(): picked_rows = top_solution[:, row_map]]
  transfers between devices with their start and end apart: 6 -> 0, of which waited for: 6 -> 0; matrix products, arithmetic and copies ran while one was open for 0% -> 0% of each run, Pallas kernels for 0% -> 0%
where the time goes in v2:
time: 88.4 us; the launch traced here: 88.2 us
  Pallas kernels  84.3 us (95%)
  local copies, waits for them, and re-layouts  3.34 us (4%)
    pallas_call x1, Pallas kernels, on_device(): pl.pallas_call(functools.partial(kernel, (nz, ny)), out_shape=(jax.ShapeD...  84.3 us
    unnamed x2, local copies, waits for them, and re-layouts  3.34 us

profile of v2, /device:TPU:1, one launch (start us, length us, event | category | flops | bytes accessed | tf_op | source)
XLA Modules:
  0.0 88.2 jit_solution(15268969482673307263)
XLA Ops:
  0.6 84.3 %shard_map.77 = (f32[512,128]{1,0:T(8,128)}, f32[32,2048]{1,0:T(8,128)}) custom-call(f32[512,128]{1,0:T(8,128)} %bitcast.2, f32[32,2048]{1,0:T(8,128)} %trhs_hbm.1, s32[16,128]{1,0:T(8,128)} %map_hbm.1, f32[16,128,512]{2,1,0:T(8,128)} %inv_hbm.1, f32[16,128,512]{2,1,0:T(8,128)} %below_hbm.1, f32[4,128,512]{2,1,0:T(8,128)} %tinv_hbm.1), custom_call_target="tpu_custom_call" | custom-call | flops 805306368 | bytes 10485760 | tf_op jit(solution)/shard_map/pallas_call | solution.py:598
  84.9 1.7 %copy.10 = f32[32,16,128]{2,1,0:T(8,128)} copy(f32[32,16,128]{2,1,0:T(8,128)} %bitcast.3) | data formatting | bytes 524288
  86.6 1.7 %copy.11 = f32[32,2048]{1,0:T(8,128)} copy(f32[32,2048]{1,0:T(8,128)} %get-tuple-element.9) | data formatting | bytes 524288

commit v3 on v2

--- a/solution.py
+++ b/solution.py
@@ -9,7 +9,6 @@
 
 F32 = jnp.float32
 BF16 = jnp.bfloat16
-NT_DIMS = (((1,), (1,)), ((), ()))
 NN_DIMS = (((1,), (0,)), ((), ()))
 
 NX = 4
@@ -24,8 +23,9 @@
 B_FIRST = 13
 B_AT = (0, 3, 6, 9, 12)
 B_GAP = 0
+LEAVE_AT = 5
 STRAIGHT = ((0, 0), (6, 8), (0, 0), (6, 8))
-PREP = 4
+PREP = 3
 
 
 def split(v):
@@ -53,7 +53,7 @@
     dims,
     rhs_hbm, trhs_hbm, map_hbm, inv_hbm, below_hbm, tinv_hbm,
     leaf_out, top_out,
-    rhs_ref, trhs_ref, map_ref, a_f32, b_f32, t_f32, a_hl, b_hl, t_hl, a_t, b_t, hot_in, hot_out,
+    rhs_ref, trhs_ref, map_ref, a_f32, b_f32, t_f32, a_hl, b_hl, t_hl, a_t, b_t, t_t, hot_in, hot_out,
     gb, gy, upd, urow, ztop, cbuf, yacc, ybuf, zbuf, xbuf, xbuf2, rvec, hl_in, sol, s_hl,
     pb, pa, r1b, r1a, r2b, r2a,
     in_sem, ssem, rsem, tssem, trsem,
@@ -62,8 +62,8 @@
     nodes, k = gb.shape[2], gb.shape[3]
     chunks = nodes // G
     units = H * chunks
-    nt = t_f32.shape[0]
     cols = upd.shape[2]
+    nt = cols // t_f32.shape[2]
     yrows = urow.shape[1] // ny
     prow = yrows // nz
     kp = prow // 4
@@ -77,18 +77,24 @@
     right, left = lax.rem(x + 1, NX), lax.rem(x + NX - 1, NX)
     opp = lax.rem(x + 2, NX)
 
+    first = y * yrows + z * prow
+    t_mine = lax.div(first, 4 * k)
+
     def leaf_of(zz, yy, cc):
         return (zz * ny + yy) * 2 + cc
 
-    xpeers = [lax.rem(x + d, NX) for d in range(1, NX)]
-    ypeers = [lax.rem(y + d, ny) for d in range(1, ny)]
-    zpeers = [lax.rem(z + d, nz) for d in range(1, nz)]
+    def others(n):
+        return sorted(range(1, n), key=lambda d: -min(d, n - d))
+
+    xpeers = [lax.rem(x + d, NX) for d in others(NX)]
+    ypeers = [lax.rem(y + d, ny) for d in others(ny)]
+    zpeers = [lax.rem(z + d, nz) for d in others(nz)]
     partner = leaf_of(z, y, 1 - core)
 
     barrier = pltpu.get_barrier_semaphore()
-    peers = [{"rows": p} for p in xpeers]
+    peers = [{"leaf": leaf_of(p, y, core)} for p in zpeers]
     peers += [{"leaf": leaf_of(z, p, core)} for p in ypeers]
-    peers += [{"leaf": leaf_of(p, y, core)} for p in zpeers]
+    peers += [{"rows": p} for p in xpeers]
     peers += [{"leaf": partner}]
     for p in peers:
         pl.semaphore_signal(barrier, inc=1, device_id=p, device_id_type=pl.DeviceIdType.MESH)
@@ -100,7 +106,7 @@
     whole = [
         pltpu.make_async_copy(src, dst, in_sem.at[2, i])
         for i, (src, dst) in enumerate(
-            ((rhs_hbm, rhs_ref), (map_hbm, map_ref), (tinv_hbm, t_f32), (trhs_hbm, trhs_ref))
+            ((rhs_hbm, rhs_ref), (map_hbm, map_ref), (tinv_hbm.at[pl.ds(t_mine, 1)], t_f32), (trhs_hbm, trhs_ref))
         )
     ]
     whole[0].start()
@@ -122,11 +128,6 @@
 
     lax.fori_loop(0, nodes, fill_own, 0)
 
-    def store_split(dst, n, v):
-        hi, lo = split(v)
-        dst[n, 0:LANES, :] = hi
-        dst[n, LANES : 2 * LANES, :] = lo
-
     def store_both(dst, dst_t, n, v):
         hi, lo = split(v)
         dst[n, 0:LANES, :] = hi
@@ -140,10 +141,12 @@
             store_both(a_hl, a_t, c * G + j, a_f32[c * G + j])
         return 0
 
-    def prepare_below(c, _):
+    def prepare_below(c):
         load(1, c).wait()
         for j in range(G):
             store_both(b_hl, b_t, c * G + j, b_f32[c * G + j])
+
+    def prepare_in(c, _):
         for j in range(G):
             own = jnp.broadcast_to(map_ref[pl.ds(c * G + j, 1), :], (LANES, LANES)).T
             at = lax.broadcasted_iota(jnp.int32, (LANES, LANES), 1)
@@ -233,10 +236,9 @@
     lax.fori_loop(0, chunks, start_rhs, 0)
 
     lax.fori_loop(PREP, chunks, prepare, 0)
-    lax.fori_loop(0, chunks, prepare_below, 0)
+    lax.fori_loop(0, chunks, prepare_in, 0)
     whole[2].wait()
-    for t in range(nt):
-        store_split(t_hl, t, t_f32[t])
+    store_both(t_hl, t_t, 0, t_f32[0])
     whole[3].wait()
     for t in range(nt):
         for q in range(4):
@@ -303,8 +305,6 @@
             def _():
                 hand.start()
 
-    first = y * yrows + z * prow
-    t_mine = first // (4 * k)
     ysends = [
         tsend(1, d, yacc.at[rows_at(p * yrows, yrows)], ybuf.at[d], {"leaf": leaf_of(z, p, core)})
         for d, p in enumerate(ypeers)
@@ -355,12 +355,12 @@
         hi, lo = split(r)
         hl_in[0:kp, :] = hi.astype(F32)
         hl_in[mp : mp + kp, :] = lo.astype(F32)
-        o = lax.dot_general(hl_in[...].astype(BF16), t_hl[t_mine], NT_DIMS, preferred_element_type=F32)
+        o = lax.dot_general(hl_in[...].astype(BF16), t_t[0], NN_DIMS, preferred_element_type=F32)
         f = (o[:mp, :LANES] + o[:mp, LANES:]) + (o[mp:, :LANES] + o[mp:, LANES:])
         hi, lo = split(f)
         fhl = jnp.concatenate([hi.astype(F32), lo.astype(F32)], 0)
         fhl = jnp.concatenate([fhl, fhl], 1).astype(BF16)
-        o = lax.dot_general(fhl, t_hl[t_mine], NN_DIMS, preferred_element_type=F32)
+        o = lax.dot_general(fhl, t_hl[0], NN_DIMS, preferred_element_type=F32)
         s_part = o[:mp] + o[mp:]
         for q in range(4):
             rvec[pl.ds(q, kp, stride=4), :] = s_part[0:kp, q * LANES : (q + 1) * LANES]
@@ -450,6 +450,19 @@
         toward_next(phase, u, 3).wait_recv()
         return buf[x, h, ns] + (r2[0, h, ns] + r2[1, h, ns])
 
+    def reduce_leave(phase, u):
+        toward_next(phase, u, 2).wait_send()
+        toward_next(phase, u, 3).wait_send()
+
+        @pl.when(straight(phase, u))
+        def _():
+            toward_next(phase, u, 4).wait_send()
+
+        @pl.when(jnp.logical_not(straight(phase, u)))
+        def _():
+            toward_opp(phase, u, 0).wait_send()
+            toward_opp(phase, u, 1).wait_send()
+
     def b0(u):
         h, c = place(u)
         picked = lax.dot_general(s_hl[h], hot_out[c], NN_DIMS, preferred_element_type=F32).astype(BF16)
@@ -475,6 +488,7 @@
 
     def b4(u):
         h, c = place(u)
+        reduce_leave(2, u)
         done = reduce_end(3, u)
         for j in range(G):
             leaf_out[pl.ds(h * k * nodes + c * G + j, k, stride=nodes), :] = done[j]
@@ -488,47 +502,53 @@
     base = F_AT[3] + chunks - 1
     b_base = base + B_FIRST
 
-    def step(i, _):
-        def unit_at(at, gap, body):
-            v = i - at
-            second = v >= chunks + gap
-
-            @pl.when(((v >= 0) & (v < chunks)) | (second & (v < units + gap)))
-            def _():
-                body(jnp.where(second, v - gap, v))
-
-        for j, body in enumerate((t0, t1, t2, t3, t4, t5, t6)):
-            pl.when(i == base + jnp.where(core == 0, TOP_AT[0][j], TOP_AT[1][j]))(body)
-        pl.when(i == base + jnp.where(core == 0, TAKE_AT[0], TAKE_AT[1]))(take)
-        unit_at(F_AT[0], F_GAP, f0)
-        unit_at(F_AT[2], F_GAP, f2)
-        unit_at(F_AT[1], F_GAP, f1)
-        unit_at(F_AT[3], F_GAP, f3)
-        unit_at(b_base + B_AT[1], B_GAP, b1)
-        unit_at(b_base + B_AT[3], B_GAP, b3)
-        unit_at(b_base + B_AT[4], B_GAP, b4)
-        unit_at(b_base + B_AT[2], B_GAP, b2)
-        unit_at(b_base + B_AT[0], B_GAP, b0)
-        unit_at(base + TOP_AT[0][2], 0, leave_forward)
-        pl.when((i > base) & (i <= base + chunks))(lambda: prepare_out(i - base - 1))
-        return 0
-
-    lax.fori_loop(0, b_base + B_AT[4] + units + B_GAP, step, 0)
+    tops = (t0, t1, t2, t3, t4, t5, t6)
+    forwards = ((0, f0), (2, f2), (1, f1), (3, f3))
+    backwards = ((1, b1), (3, b3), (4, b4), (2, b2), (0, b0))
+
+    def run(low, high):
+        def holds(at, gap):
+            return at < high and at + units + gap > low
+
+        def step(i, _):
+            def unit_at(at, gap, body):
+                v = i - at
+                second = v >= chunks + gap
+
+                @pl.when(((v >= 0) & (v < chunks)) | (second & (v < units + gap)))
+                def _():
+                    body(jnp.where(second, v - gap, v))
+
+            def when_at(ats, body):
+                for c, at in enumerate(ats):
+                    if low <= base + at < high:
+                        pl.when((core == c) & (i == base + at))(body)
+
+            for j, body in enumerate(tops):
+                when_at((TOP_AT[0][j], TOP_AT[1][j]), body)
+            when_at(TAKE_AT, take)
+            for j, body in forwards:
+                if holds(F_AT[j], F_GAP):
+                    unit_at(F_AT[j], F_GAP, body)
+                if j == 0 and low == 0:
+                    pl.when(i < chunks)(lambda: prepare_below(i))
+            if holds(base + 1, 0):
+                pl.when((i > base) & (i <= base + chunks))(lambda: prepare_out(i - base - 1))
+            if holds(base + LEAVE_AT, 0):
+                unit_at(base + LEAVE_AT, 0, leave_forward)
+            for j, body in backwards:
+                if holds(b_base + B_AT[j], B_GAP):
+                    unit_at(b_base + B_AT[j], B_GAP, body)
+            return 0
+
+        lax.fori_loop(low, high, step, 0)
+
+    run(0, base + 1)
+    run(base + 1, b_base)
+    run(b_base, b_base + B_AT[4] + units + B_GAP)
 
     def drain(u, _):
-        for phase in (2, 3):
-            toward_next(phase, u, 2).wait_send()
-            toward_next(phase, u, 3).wait_send()
-
-            @pl.when(straight(phase, u))
-            def _(phase=phase):
-                toward_next(phase, u, 4).wait_send()
-
-            @pl.when(jnp.logical_not(straight(phase, u)))
-            def _(phase=phase):
-                toward_opp(phase, u, 0).wait_send()
-                toward_opp(phase, u, 1).wait_send()
-
+        reduce_leave(3, u)
         return 0
 
     lax.fori_loop(0, units, drain, 0)
@@ -539,7 +559,7 @@
 def make(nz, ny):
     def on_device(leaf_rhs, top_rhs, leaf_inverse, leaf_below, row_map, top_inverse):
         k, nodes, width = leaf_rhs.shape
-        nt, _, s = top_inverse.shape
+        s = top_inverse.shape[2]
         full = leaf_inverse.shape[2]
         cols = top_rhs.shape[1]
         chunks = nodes // G
@@ -559,12 +579,13 @@
             pltpu.VMEM((nodes, width), jnp.int32),
             pltpu.VMEM(leaf_inverse.shape, F32),
             pltpu.VMEM(leaf_below.shape, F32),
-            pltpu.VMEM(top_inverse.shape, F32),
+            pltpu.VMEM((1,) + top_inverse.shape[1:], F32),
             pltpu.VMEM((nodes, 2 * LANES, full), BF16),
             pltpu.VMEM((nodes, 2 * LANES, full), BF16),
-            pltpu.VMEM((nt, 2 * LANES, s), BF16),
+            pltpu.VMEM((1, 2 * LANES, s), BF16),
             pltpu.VMEM((nodes, full, 2 * LANES), BF16),
             pltpu.VMEM((nodes, full, 2 * LANES), BF16),
+            pltpu.VMEM((1, s, 2 * LANES), BF16),
             pltpu.VMEM((chunks, G * LANES, cols), BF16),
             pltpu.VMEM((chunks, cols, G * LANES), BF16),
             pltpu.VMEM(blocks, F32),

time: 88.4 us -> 86.7 us (0.981)
  Pallas kernels: 84.3 us -> 82.5 us
    pallas_call x1, Pallas kernels: 84.3 us -> 82.5 us  [on_device(): pl.pallas_call(functools.partial(kernel, (nz, ny)), out_shape=(jax.ShapeD...]
where the time goes in v3:
time: 86.7 us; the launch traced here: 86.5 us
  Pallas kernels  82.5 us (95%)
  local copies, waits for them, and re-layouts  3.34 us (4%)
    pallas_call x1, Pallas kernels, on_device(): pl.pallas_call(functools.partial(kernel, (nz, ny)), out_shape=(jax.ShapeD...  82.5 us
    unnamed x2, local copies, waits for them, and re-layouts  3.34 us

profile of v3, /device:TPU:1, one launch (start us, length us, event | category | flops | bytes accessed | tf_op | source)
XLA Modules:
  0.0 86.5 jit_solution(5810990541145645545)
XLA Ops:
  0.6 82.5 %shard_map.77 = (f32[512,128]{1,0:T(8,128)}, f32[32,2048]{1,0:T(8,128)}) custom-call(f32[512,128]{1,0:T(8,128)} %bitcast.2, f32[32,2048]{1,0:T(8,128)} %trhs_hbm.1, s32[16,128]{1,0:T(8,128)} %map_hbm.1, f32[16,128,512]{2,1,0:T(8,128)} %inv_hbm.1, f32[16,128,512]{2,1,0:T(8,128)} %below_hbm.1, f32[4,128,512]{2,1,0:T(8,128)} %tinv_hbm.1), custom_call_target="tpu_custom_call" | custom-call | flops 805306368 | bytes 10485760 | tf_op jit(solution)/shard_map/pallas_call | solution.py:619
  83.2 1.7 %copy.10 = f32[32,16,128]{2,1,0:T(8,128)} copy(f32[32,16,128]{2,1,0:T(8,128)} %bitcast.3) | data formatting | bytes 524288
  84.8 1.7 %copy.11 = f32[32,2048]{1,0:T(8,128)} copy(f32[32,2048]{1,0:T(8,128)} %get-tuple-element.9) | data formatting | bytes 524288
